TPU v7x, 32 devices: a whole 2x2x4 slice. The times are simulated.
32 devices in a mesh: sensor: 16 (over z, y, core), day: 2 (over x).
Axes of the slice: x: 2, y: 2, z: 4, core: 2. Of those that a mesh axis runs over, the one named last changes fastest.
Arguments:
- y_obs: bfloat16 [2880, 2048], P('day', 'sensor'), may hold values from -256 to 256
- observed: int32 [2880, 2048], P('day', 'sensor'), may hold values 0 or 1
- day_factor: bfloat16 [10, 64], P('day'), may hold values from -6 to 6
- slot_factor: bfloat16 [288, 64], P('day'), may hold values from -6 to 6
- sensor_factor: bfloat16 [64, 2048], P(None, 'sensor'), may hold values from -6 to 6
- prior_scale: float32 [64], replicated, may hold values from 0.5 to 2
- neighbours: int32 [6, 2048], P(None, 'sensor'), may hold values from 0 to 2047, as said below
- edge_weight: float32 [6, 2048], P(None, 'sensor'), may hold values from 0.2 to 1
- noise: float32 [64, 2048], P(None, 'sensor'), may hold values from -6 to 6
Outputs:
- fresh_factor: float32 [64, 2048], P(None, 'sensor')
Inputs may be any that keep to these rules, and one draw needn't show every extreme that they name: Each sensor's neighbours are other sensors within 256 of it in index; its first two lie exactly that far away.
All inputs are finite; a program needn't handle non-finite values. No bound on the sum of `observed` on one device may be relied on, other than what follows from the above.
Results may differ from a plain program's by a relative error of at most 0.0023.
Values may be sent and summed in bfloat16 or wider, within the bound.
A program may use at most 64 MiB of HBM per device.

v0:
```python
import functools

import jax
import jax.numpy as jnp
from jax import lax
from jax.experimental import pallas as pl
from jax.experimental.pallas import tpu as pltpu
from jax.sharding import PartitionSpec as P

RANK = 64
LANES = 128
HALF = 64
BLOCKS = RANK // 8
VMEM_BYTES = 60 * 1024 * 1024


def lane_low(shape):
    return lax.broadcasted_iota(jnp.int32, shape, len(shape) - 1) < HALF


def both_halves(tile, upper):
    other = pltpu.roll(tile, HALF, 1)
    low = lane_low(tile.shape)
    return jnp.where(low, other, tile) if upper else jnp.where(low, tile, other)


def row_of(tile, index):
    return jnp.broadcast_to(tile[index : index + 1, :], tile.shape)


def factor_and_solve(load_columns, target, noise_tile, cols, wide, inv_diag, halfway, found):
    target = list(target)
    for block in range(BLOCKS):
        first = block // 2
        upper = block % 2 == 1
        count = 4 - first
        columns = load_columns(block)
        if block > 0:

            def subtract(k, carry):
                done = [cols[k, pl.ds(8 * q, 8), :] for q in range(first, 4)]
                out = []
                for c in range(8):
                    scale = jnp.broadcast_to(wide[k, pl.ds(8 * block + c, 1), :], (8, LANES))
                    out.extend(carry[c * count + q] - done[q] * scale for q in range(count))
                return tuple(out)

            flat = tuple(tile for column in columns for tile in column)
            flat = lax.fori_loop(0, 8 * block, subtract, flat, unroll=2)
            columns = [list(flat[c * count : (c + 1) * count]) for c in range(8)]
        corner = [both_halves(column[0], upper) for column in columns]
        side = both_halves(target[first], upper)
        for c in range(8):
            j = 8 * block + c
            inverse = lax.rsqrt(row_of(corner[c], c))
            corner[c] = corner[c] * inverse
            columns[c] = [tile * inverse for tile in columns[c]]
            solved = row_of(side, c) * inverse
            side = side - corner[c] * solved
            for q in range(count):
                target[first + q] = target[first + q] - columns[c][q] * solved
            for later in range(c + 1, 8):
                scale = row_of(corner[c], later)
                corner[later] = corner[later] - corner[c] * scale
                columns[later] = [
                    tile - own * scale for tile, own in zip(columns[later], columns[c])
                ]
            inv_diag[j] = inverse
            halfway[pl.ds(j, 1), :] = solved[0:1, :]
        for c in range(8):
            j = 8 * block + c
            for q in range(count):
                tile = columns[c][q]
                row = 16 * (first + q)
                cols[j, pl.ds(8 * (first + q), 8), :] = tile
                if row >= 8 * block:
                    wide[j, pl.ds(row, 8), :] = both_halves(tile, False)
                wide[j, pl.ds(row + 8, 8), :] = both_halves(tile, True)

    packed = [None] * 4
    low = lane_low((8, LANES))
    below = None
    for block in reversed(range(BLOCKS)):
        first = block // 2
        upper = block % 2 == 1
        right = halfway[pl.ds(8 * block, 8), :] + noise_tile(block)
        remain = []
        for c in range(8):
            j = 8 * block + c
            total = row_of(right, c)
            parts = None
            for q in range(first, 4):
                if q == first and upper:
                    continue
                if q == first:
                    term = jnp.where(low, 0.0, cols[j, pl.ds(8 * q, 8), :] * below)
                else:
                    term = cols[j, pl.ds(8 * q, 8), :] * packed[q]
                parts = term if parts is None else parts + term
            if parts is not None:
                sums = jnp.sum(parts, axis=0, keepdims=True)
                sums = jnp.broadcast_to(sums, (8, LANES))
                total = total - (sums + pltpu.roll(sums, HALF, 1))
            remain.append(total)
        values = [None] * 8
        for c in reversed(range(8)):
            values[c] = remain[c] * inv_diag[8 * block + c]
            for earlier in range(c):
                scale = jnp.broadcast_to(
                    wide[8 * block + earlier, pl.ds(8 * block + c, 1), :], (8, LANES)
                )
                remain[earlier] = remain[earlier] - scale * values[c]
        rows = lax.broadcasted_iota(jnp.int32, (8, LANES), 0)
        tile = values[0]
        for c in range(1, 8):
            tile = jnp.where(rows == c, values[c], tile)
        found[pl.ds(8 * block, 8), :] = tile
        if upper:
            below = tile
        else:
            packed[first] = jnp.where(low, tile, below)
            below = None
    return packed


def diagonal_tile(block, c, value):
    shape = (8, LANES)
    rows = lax.broadcasted_iota(jnp.int32, shape, 0)
    low = lane_low(shape)
    half = low if block % 2 == 0 else jnp.logical_not(low)
    return jnp.where((rows == c) & half, value, 0.0)


def solve_kernel(squares, target, noise, prior, out, cols, wide, inv_diag, halfway):
    def load_columns(block):
        first = block // 2
        own = prior[pl.ds(8 * block, 8), :]
        columns = []
        for c in range(8):
            j = 8 * block + c
            tiles = [squares[j, pl.ds(8 * q, 8), :] for q in range(first, 4)]
            tiles[0] = tiles[0] + diagonal_tile(block, c, own)
            columns.append(tiles)
        return columns

    targets = [target[pl.ds(8 * q, 8), :] for q in range(4)]
    factor_and_solve(
        load_columns,
        targets,
        lambda block: noise[pl.ds(8 * block, 8), :],
        cols,
        wide,
        inv_diag,
        halfway,
        out,
    )


def solver_scratch():
    return [
        pltpu.VMEM((RANK, 32, LANES), jnp.float32),
        pltpu.VMEM((RANK, RANK, LANES), jnp.float32),
        pltpu.VMEM((RANK, 8, LANES), jnp.float32),
        pltpu.VMEM((RANK, LANES), jnp.float32),
    ]


def pack_rows(rows):
    lead = rows.shape[:-2]
    split = rows.reshape(lead + (4, 2, 8, HALF))
    return jnp.swapaxes(split, -3, -2).reshape(lead + (32, LANES))


def solve_block(gram, right, pulled, prior_diag, prior_scale, noise, tau):
    share = right.shape[1]

    def fill(array, value=0.0):
        pad = [(0, 0)] * (array.ndim - 1) + [(0, HALF - share)]
        return jnp.pad(array, pad, constant_values=value)

    target = tau * right + prior_scale[:, None] * pulled
    prior = prior_scale[:, None] * fill(prior_diag, 1.0)[None, :]
    twice = lambda array: jnp.concatenate([array, array], axis=1)
    spec = pl.BlockSpec(memory_space=pltpu.VMEM)
    solved = pl.pallas_call(
        solve_kernel,
        out_shape=jax.ShapeDtypeStruct((RANK, LANES), jnp.float32),
        in_specs=[spec] * 4,
        out_specs=spec,
        scratch_shapes=solver_scratch(),
        compiler_params=pltpu.CompilerParams(vmem_limit_bytes=24 * 1024 * 1024),
        name="solve_sensors",
    )(tau * pack_rows(fill(gram)), pack_rows(fill(target)), twice(fill(noise)), twice(prior))
    return solved[:, :share]


def shifted(shard, axis, by):
    size = lax.axis_size(axis)
    pairs = [(i, i + by) for i in range(size) if 0 <= i + by < size]
    return lax.ppermute(shard, axis, pairs)


def general_shards(
    y_obs,
    observed,
    day_factor,
    slot_factor,
    sensor_factor,
    prior_scale,
    neighbours,
    edge_weight,
    noise,
):
    rank = sensor_factor.shape[0]
    block_len = sensor_factor.shape[1]
    all_slots = lax.all_gather(slot_factor, "day", axis=0, tiled=True)
    features = (day_factor[:, None, :] * all_slots[None, :, :]).reshape(-1, rank)
    row_total = features.shape[0] * lax.axis_size("day")
    outer_rows = (features[:, :, None] * features[:, None, :]).reshape(-1, rank * rank)
    mask_half = observed.astype(jnp.bfloat16)
    weighted = mask_half * y_obs
    dims = (((0,), (0,)), ((), ()))
    gram_sums = lax.dot_general(outer_rows, mask_half, dims, preferred_element_type=jnp.float32)
    right_sums = lax.dot_general(features, weighted, dims, preferred_element_type=jnp.float32)
    pieces = []
    for offset in (2, 1, 0, -1, -2):
        if offset == 0:
            pieces.append(sensor_factor)
        else:
            pieces.append(shifted(sensor_factor, "sensor", offset))
    window = jnp.concatenate(pieces, axis=1)
    base_col = (lax.axis_index("sensor") - 2) * block_len
    columns = neighbours - base_col
    picked = jnp.take(window, columns, axis=1).astype(jnp.float32)
    pulled = jnp.einsum("rns,ns->rs", picked, edge_weight)
    prior_diag = 1.0 + jnp.sum(edge_weight, axis=0)
    tau = 4.0 / row_total
    sums = jnp.concatenate([gram_sums, right_sums], axis=0)
    sums = lax.psum_scatter(sums, "day", scatter_dimension=1, tiled=True)
    share_len = sums.shape[1]
    first_col = lax.axis_index("day") * share_len
    part = lambda array: lax.dynamic_slice_in_dim(array, first_col, share_len, array.ndim - 1)
    solved = solve_block(
        sums[: rank * rank].reshape(rank, rank, share_len),
        sums[rank * rank :],
        part(pulled),
        part(prior_diag),
        prior_scale,
        part(noise),
        tau,
    )
    return lax.all_gather(solved, "day", axis=1, tiled=True)


COUNTS = [4 - block // 2 for block in range(BLOCKS)]
STARTS = [64 * sum(COUNTS[:block]) for block in range(BLOCKS)]
PACKED_ROWS = 64 * sum(COUNTS)
OFFSETS = (-2, -1, 1, 2)
DAY_ROWS = 16


def pack_pair(even, odd, own):
    low = lane_low(even.shape)
    if own:
        return jnp.where(low, even, pltpu.roll(odd, HALF, 1))
    return jnp.where(low, pltpu.roll(even, HALF, 1), odd)


def split_pairs(rows):
    count = rows.shape[0] // 16
    pairs = rows.reshape(count, 2, 8, LANES)
    return pairs[:, 0].reshape(8 * count, LANES), pairs[:, 1].reshape(8 * count, LANES)


def sweep_kernel(
    tau,
    days,
    y_hbm,
    observed_hbm,
    day_hbm,
    slot_hbm,
    factor_hbm,
    scale_hbm,
    neighbour_hbm,
    weight_hbm,
    noise_hbm,
    out_ref,
    day_ref,
    slot_ref,
    factor_ref,
    scale_ref,
    neighbour_ref,
    weight_ref,
    noise_ref,
    y_ref,
    observed_ref,
    mask_ref,
    weighted_ref,
    sent_mask,
    got_mask,
    sent_weighted,
    got_weighted,
    slot_wide,
    sent_factors,
    got_factors,
    window,
    features,
    wide_features,
    half_features,
    outer,
    gram,
    prior_ref,
    noise_own,
    packed_ref,
    peer_packed,
    found,
    cols,
    wide,
    inv_diag,
    halfway,
    load_sems,
    factor_sems,
    mask_sems,
    weighted_sems,
    window_send,
    window_recv,
    final_sems,
):
    day = lax.axis_index("day")
    sensor = lax.axis_index("sensor")
    sensors = lax.axis_size("sensor")
    rows = y_ref.shape[0]
    half_rows = rows // 2
    padded = mask_ref.shape[1]
    half_slots = slot_ref.shape[1]
    peer = {"day": 1 - day}
    mesh_id = pl.DeviceIdType.MESH
    f32, bf16 = jnp.float32, jnp.bfloat16

    barrier = pltpu.get_barrier_semaphore()
    pl.semaphore_signal(barrier, inc=1, device_id=peer, device_id_type=mesh_id)
    others = [lax.rem(sensor + sensors + offset, sensors) for offset in OFFSETS]
    for other in others:
        pl.semaphore_signal(barrier, inc=1, device_id={"sensor": other}, device_id_type=mesh_id)
    pairs = (
        (slot_hbm, slot_ref),
        (day_hbm, day_ref),
        (observed_hbm, observed_ref),
        (y_hbm, y_ref),
        (factor_hbm, factor_ref),
        (scale_hbm, scale_ref),
        (neighbour_hbm, neighbour_ref),
        (weight_hbm, weight_ref),
        (noise_hbm, noise_ref),
    )
    loads = []
    for index, (source, target) in enumerate(pairs):
        load = pltpu.make_async_copy(source, target, load_sems.at[index])
        load.start()
        loads.append(load)
    load_slots, load_days, load_mask, load_y, load_factor = loads[:5]

    def to_peer(source, target, sems):
        return pltpu.make_async_remote_copy(
            src_ref=source,
            dst_ref=target,
            send_sem=sems.at[0],
            recv_sem=sems.at[1],
            device_id=peer,
            device_id_type=mesh_id,
        )

    slot_wide[...] = jnp.zeros(slot_wide.shape, f32)
    load_slots.wait()
    slot_wide[pl.ds(0, RANK), pl.ds(0, half_slots)] = slot_ref[...].astype(f32)
    here = slot_wide[...].T[:half_slots]
    sent_factors[pl.ds(0, half_slots), :] = here.astype(bf16)
    load_days.wait()
    day_own = day_ref[...].astype(f32)
    day_own = jnp.concatenate([day_own, day_own], axis=1)
    tile_rows = lax.broadcasted_iota(jnp.int32, (DAY_ROWS, LANES), 0)
    day_tile = jnp.zeros((DAY_ROWS, LANES), f32)
    for index in range(days):
        day_tile = jnp.where(tile_rows == index, day_own[index : index + 1, :], day_tile)
    sent_factors[pl.ds(half_slots, DAY_ROWS), :] = day_tile.astype(bf16)

    def own_first(tile):
        return jnp.where(day == 0, tile, pltpu.roll(tile, HALF, 1))

    load_mask.wait()
    mask = own_first(observed_ref[...].astype(f32))
    mask_ref[0, pl.ds(0, rows), :] = mask.astype(bf16)
    sent_mask[...] = pack_pair(mask[:half_rows], mask[half_rows:], False).astype(bf16)

    load_factor.wait()
    pl.semaphore_wait(barrier, 1 + len(OFFSETS))
    factor_copy = to_peer(sent_factors, got_factors, factor_sems)
    factor_copy.start()
    mask_copy = to_peer(sent_mask, got_mask, mask_sems)
    mask_copy.start()
    window_copies = []
    for index, (offset, other) in enumerate(zip(OFFSETS, others)):
        copy = pltpu.make_async_remote_copy(
            src_ref=factor_ref,
            dst_ref=window.at[2 - offset],
            send_sem=window_send.at[index],
            recv_sem=window_recv.at[index],
            device_id={"sensor": other},
            device_id_type=mesh_id,
        )
        copy.start()
        window_copies.append(copy)

    load_y.wait()
    weighted = own_first(observed_ref[...].astype(f32) * y_ref[...].astype(f32))
    weighted_ref[0, pl.ds(0, rows), :] = weighted.astype(bf16)
    sent_weighted[...] = pack_pair(weighted[:half_rows], weighted[half_rows:], False).astype(bf16)
    weighted_copy = to_peer(sent_weighted, got_weighted, weighted_sems)
    weighted_copy.start()
    if padded > rows:
        empty = jnp.zeros((padded - rows, LANES), bf16)
        for part in range(2):
            mask_ref[part, pl.ds(rows, padded - rows), :] = empty
            weighted_ref[part, pl.ds(rows, padded - rows), :] = empty
        features[pl.ds(rows, padded - rows), :] = jnp.zeros((padded - rows, LANES), f32)

    factor_copy.wait()
    there = got_factors[pl.ds(0, half_slots), :].astype(f32)
    early = jnp.where(day == 0, here, there)
    late = jnp.where(day == 0, there, here)
    day_peer = got_factors[pl.ds(half_slots, DAY_ROWS), :].astype(f32)

    def make_features(part):
        day_rows = day_own if part == 0 else day_peer
        for index in range(days):
            row = day_rows[index : index + 1, :]
            at = index * 2 * half_slots
            features[pl.ds(at, half_slots), :] = early * row
            features[pl.ds(at + half_slots, half_slots), :] = late * row
        for index in range(padded // LANES):
            piece = features[pl.ds(index * LANES, LANES), :].T[:RANK]
            rounded = piece.astype(bf16)
            half_features[part, :, pl.ds(index * LANES, LANES)] = rounded
            wide_features[part, :, pl.ds(index * LANES, LANES)] = rounded.astype(f32)

    def gram_block(part, block):
        first = block // 2
        count = COUNTS[block]
        slab = outer.at[block % 2]
        for c in range(8):
            row = wide_features[part, pl.ds(8 * block + c, 1), :]
            row = jnp.broadcast_to(row, (16, padded)).astype(bf16)
            for q in range(first, 4):
                at = 16 * (c * count + q - first)
                slab[pl.ds(at, 16), :] = half_features[part, pl.ds(16 * q, 16), :] * row
        sums = jnp.dot(slab[pl.ds(0, 128 * count), :], mask_ref[part], preferred_element_type=f32)
        even, odd = split_pairs(sums)
        return pack_pair(even, odd, True)

    make_features(0)
    for block in range(BLOCKS):
        gram[pl.ds(STARTS[block], 64 * COUNTS[block]), :] = gram_block(0, block)
    make_features(1)

    for load in loads[5:]:
        load.wait()

    mine = (lax.broadcasted_iota(jnp.int32, (RANK, LANES), 1) >= HALF) == (day == 1)

    def spread_own(tile):
        return jnp.where(mine, tile, pltpu.roll(tile, HALF, 1))

    eye_rows = lax.broadcasted_iota(jnp.int32, (RANK, RANK), 0)
    eye_cols = lax.broadcasted_iota(jnp.int32, (RANK, RANK), 1)
    scale_row = jnp.broadcast_to(scale_ref[...], (RANK, RANK))
    scale = jnp.sum(jnp.where(eye_rows == eye_cols, scale_row, 0.0), axis=1, keepdims=True)
    scale = jnp.broadcast_to(scale, (RANK, LANES))
    prior_diag = 1.0 + jnp.sum(weight_ref[...], axis=0, keepdims=True)
    prior_ref[...] = scale * spread_own(jnp.broadcast_to(prior_diag, (RANK, LANES)))
    noise_own[...] = spread_own(noise_ref[...])

    base = (sensor - 2) * LANES
    column = neighbour_ref[...] - base
    weights = weight_ref[...]
    pulled = jnp.zeros((RANK, LANES), f32)
    for copy in window_copies:
        copy.wait()
    for slot in range(5):
        ids = lax.broadcasted_iota(jnp.int32, (LANES, LANES), 0) + slot * LANES
        picks = jnp.zeros((LANES, LANES), f32)
        for n in range(neighbour_ref.shape[0]):
            picks = picks + jnp.where(ids == column[n : n + 1, :], weights[n : n + 1, :], 0.0)
        high = picks.astype(bf16)
        low_part = (picks - high.astype(f32)).astype(bf16)
        source = factor_ref[...] if slot == 2 else window[slot]
        pulled = pulled + jnp.dot(source, high, preferred_element_type=f32)
        pulled = pulled + jnp.dot(source, low_part, preferred_element_type=f32)
    pulled = scale * spread_own(pulled)
    even, odd = split_pairs(pulled)
    pulled = jnp.where(lane_low(even.shape), even, odd)

    def unpack(packed, target):
        target[1, pl.ds(0, half_rows), :] = packed[...]
        turned = pltpu.roll(packed[...].astype(f32), HALF, 1)
        target[1, pl.ds(half_rows, half_rows), :] = turned.astype(bf16)

    mask_copy.wait()
    unpack(got_mask, mask_ref)
    for block in range(BLOCKS):
        at = pl.ds(STARTS[block], 64 * COUNTS[block])
        gram[at, :] = tau * (gram[at, :] + gram_block(1, block))

    weighted_copy.wait()
    unpack(got_weighted, weighted_ref)
    right = jnp.dot(half_features[0], weighted_ref[0], preferred_element_type=f32)
    right = right + jnp.dot(half_features[1], weighted_ref[1], preferred_element_type=f32)
    even, odd = split_pairs(right)
    target = tau * pack_pair(even, odd, True) + pulled

    def load_columns(block):
        first = block // 2
        count = COUNTS[block]
        prior = prior_ref[pl.ds(8 * block, 8), :]
        columns = []
        for c in range(8):
            tiles = []
            for q in range(first, 4):
                tiles.append(gram[pl.ds(STARTS[block] + 8 * (c * count + q - first), 8), :])
            tiles[0] = tiles[0] + diagonal_tile(block, c, prior)
            columns.append(tiles)
        return columns

    packed = factor_and_solve(
        load_columns,
        [target[8 * q : 8 * q + 8, :] for q in range(4)],
        lambda block: noise_own[pl.ds(8 * block, 8), :],
        cols,
        wide,
        inv_diag,
        halfway,
        found,
    )
    for q in range(4):
        packed_ref[pl.ds(8 * q, 8), :] = packed[q]
    final_copy = to_peer(packed_ref, peer_packed, final_sems)
    final_copy.start()
    final_copy.wait()
    mine_tile = (lax.broadcasted_iota(jnp.int32, (8, LANES), 1) >= HALF) == (day == 1)
    for tile in range(8):
        theirs = both_halves(peer_packed[pl.ds(8 * (tile // 2), 8), :], tile % 2 == 1)
        at = pl.ds(8 * tile, 8)
        out_ref[at, :] = jnp.where(mine_tile, found[at, :], theirs)


def paired_shards(
    y_obs,
    observed,
    day_factor,
    slot_factor,
    sensor_factor,
    prior_scale,
    neighbours,
    edge_weight,
    noise,
):
    rows = y_obs.shape[0]
    padded = -(-rows // 256) * 256
    half_slots = slot_factor.shape[0]
    slot_lanes = -(-half_slots // LANES) * LANES
    days = day_factor.shape[0]
    tau = 4.0 / (2 * rows)
    vmem = pl.BlockSpec(memory_space=pltpu.VMEM)
    hbm = pl.BlockSpec(memory_space=pl.ANY)
    f32, bf16 = jnp.float32, jnp.bfloat16
    dma = pltpu.SemaphoreType.DMA
    return pl.pallas_call(
        functools.partial(sweep_kernel, tau, days),
        out_shape=pltpu.VMEM((RANK, LANES), f32),
        in_specs=[hbm] * 9,
        out_specs=vmem,
        scratch_shapes=[
            pltpu.VMEM(day_factor.shape, bf16),
            pltpu.VMEM((RANK, half_slots), bf16),
            pltpu.VMEM((RANK, LANES), bf16),
            pltpu.VMEM((1, RANK), f32),
            pltpu.VMEM(neighbours.shape, jnp.int32),
            pltpu.VMEM(edge_weight.shape, f32),
            pltpu.VMEM((RANK, LANES), f32),
            pltpu.VMEM((rows, LANES), bf16),
            pltpu.VMEM((rows, LANES), jnp.int32),
            pltpu.VMEM((2, padded, LANES), bf16),
            pltpu.VMEM((2, padded, LANES), bf16),
            pltpu.VMEM((rows // 2, LANES), bf16),
            pltpu.VMEM((rows // 2, LANES), bf16),
            pltpu.VMEM((rows // 2, LANES), bf16),
            pltpu.VMEM((rows // 2, LANES), bf16),
            pltpu.VMEM((LANES, slot_lanes), f32),
            pltpu.VMEM((half_slots + DAY_ROWS, LANES), bf16),
            pltpu.VMEM((half_slots + DAY_ROWS, LANES), bf16),
            pltpu.VMEM((5, RANK, LANES), bf16),
            pltpu.VMEM((padded, LANES), f32),
            pltpu.VMEM((2, RANK, padded), f32),
            pltpu.VMEM((2, RANK, padded), bf16),
            pltpu.VMEM((2, 512, padded), bf16),
            pltpu.VMEM((PACKED_ROWS, LANES), f32),
            pltpu.VMEM((RANK, LANES), f32),
            pltpu.VMEM((RANK, LANES), f32),
            pltpu.VMEM((32, LANES), f32),
            pltpu.VMEM((32, LANES), f32),
            pltpu.VMEM((RANK, LANES), f32),
        ]
        + solver_scratch()
        + [dma((9,)), dma((2,)), dma((2,)), dma((2,)), dma((4,)), dma((4,)), dma((2,))],
        compiler_params=pltpu.CompilerParams(
            collective_id=0, has_side_effects=True, vmem_limit_bytes=VMEM_BYTES
        ),
        name="sweep_sensors",
    )(
        y_obs,
        observed,
        day_factor,
        slot_factor.T,
        sensor_factor,
        prior_scale.reshape(1, RANK),
        neighbours,
        edge_weight,
        noise,
    )


def solution(mesh):
    sizes = dict(mesh.shape)

    def shards(*arrays):
        y_obs, slot_factor = arrays[0], arrays[3]
        fits = sizes["day"] == 2 and sizes["sensor"] >= 5 and y_obs.shape[1] == LANES
        fits = fits and y_obs.shape[0] % 32 == 0 and slot_factor.shape[0] % 16 == 0
        fits = fits and arrays[2].shape[0] <= DAY_ROWS
        return paired_shards(*arrays) if fits else general_shards(*arrays)

    return jax.shard_map(
        shards,
        mesh=mesh,
        in_specs=(
            P("day", "sensor"),
            P("day", "sensor"),
            P("day", None),
            P("day", None),
            P(None, "sensor"),
            P(),
            P(None, "sensor"),
            P(None, "sensor"),
            P(None, "sensor"),
        ),
        out_specs=P(None, "sensor"),
        check_vma=False,
    )
```

profile of v0, /device:TPU:0, one launch (start us, length us, event | category | flops | bytes accessed | tf_op | source)
XLA Modules:
  0.0 24.4 jit_solution(4738792454957276264)
XLA Ops:
  0.0 23.8 %sweep_sensors.1 = f32[64,128]{1,0:T(8,128)S(1)} custom-call(bf16[1440,128]{1,0:T(8,128)(2,1)} %y_hbm.1, s32[1440,128]{1,0:T(8,128)} %observed_hbm.1, bf16[5,64]{1,0:T(8,128)(2,1)} %day_hbm.1, bf16[64,144]{1,0:T(8,128)(2,1)} %bitcast.2, bf16[64,128]{1,0:T(8,128)(2,1)} %factor_hbm.1, f32[1,64]{1,0:T(1,128)} %bitcast.3, s32[6,128]{1,0:T(8,128)} %neighbour_hbm.1, ...), custom_call_target="tpu_custom_call" | custom-call | tf_op jit(solution)/shard_map/sweep_sensors/pallas_call | solution.py:576
  23.8 0.6 %copy.11 = f32[64,128]{1,0:T(8,128)} copy(f32[64,128]{1,0:T(8,128)S(1)} %sweep_sensors.1) | data formatting | bytes 65536
where the time goes:
time: 24.5 us; the launch traced here: 24.4 us
  Pallas kernels  23.8 us (97%)
  local copies, waits for them, and re-layouts  0.62 us (3%)
    pallas_call x1, Pallas kernels, paired_shards(): pl.pallas_call(functools.partial(sweep_kernel, tau, days), out_shape=pltp...  23.8 us
    unnamed x1, local copies, waits for them, and re-layouts  0.62 us

commit v1 on v0

--- a/solution.py
+++ b/solution.py
@@ -298,8 +298,9 @@
     weighted_ref,
     sent_mask,
     got_mask,
-    sent_weighted,
-    got_weighted,
+    own_right,
+    sent_right,
+    got_right,
     slot_wide,
     sent_factors,
     got_factors,
@@ -321,7 +322,7 @@
     load_sems,
     factor_sems,
     mask_sems,
-    weighted_sems,
+    right_sems,
     window_send,
     window_recv,
     final_sems,
@@ -413,15 +414,12 @@
 
     load_y.wait()
     weighted = own_first(observed_ref[...].astype(f32) * y_ref[...].astype(f32))
-    weighted_ref[0, pl.ds(0, rows), :] = weighted.astype(bf16)
-    sent_weighted[...] = pack_pair(weighted[:half_rows], weighted[half_rows:], False).astype(bf16)
-    weighted_copy = to_peer(sent_weighted, got_weighted, weighted_sems)
-    weighted_copy.start()
+    weighted_ref[pl.ds(0, rows), :] = weighted.astype(bf16)
     if padded > rows:
         empty = jnp.zeros((padded - rows, LANES), bf16)
         for part in range(2):
             mask_ref[part, pl.ds(rows, padded - rows), :] = empty
-            weighted_ref[part, pl.ds(rows, padded - rows), :] = empty
+        weighted_ref[pl.ds(rows, padded - rows), :] = empty
         features[pl.ds(rows, padded - rows), :] = jnp.zeros((padded - rows, LANES), f32)
 
     factor_copy.wait()
@@ -458,6 +456,12 @@
         return pack_pair(even, odd, True)
 
     make_features(0)
+    right = jnp.dot(half_features[0], weighted_ref[...], preferred_element_type=f32)
+    even, odd = split_pairs(right)
+    own_right[...] = pack_pair(even, odd, True)
+    sent_right[...] = pack_pair(even, odd, False)
+    right_copy = to_peer(sent_right, got_right, right_sems)
+    right_copy.start()
     for block in range(BLOCKS):
         gram[pl.ds(STARTS[block], 64 * COUNTS[block]), :] = gram_block(0, block)
     make_features(1)
@@ -499,23 +503,16 @@
     even, odd = split_pairs(pulled)
     pulled = jnp.where(lane_low(even.shape), even, odd)
 
-    def unpack(packed, target):
-        target[1, pl.ds(0, half_rows), :] = packed[...]
-        turned = pltpu.roll(packed[...].astype(f32), HALF, 1)
-        target[1, pl.ds(half_rows, half_rows), :] = turned.astype(bf16)
-
     mask_copy.wait()
-    unpack(got_mask, mask_ref)
+    mask_ref[1, pl.ds(0, half_rows), :] = got_mask[...]
+    turned = pltpu.roll(got_mask[...].astype(f32), HALF, 1)
+    mask_ref[1, pl.ds(half_rows, half_rows), :] = turned.astype(bf16)
     for block in range(BLOCKS):
         at = pl.ds(STARTS[block], 64 * COUNTS[block])
         gram[at, :] = tau * (gram[at, :] + gram_block(1, block))
 
-    weighted_copy.wait()
-    unpack(got_weighted, weighted_ref)
-    right = jnp.dot(half_features[0], weighted_ref[0], preferred_element_type=f32)
-    right = right + jnp.dot(half_features[1], weighted_ref[1], preferred_element_type=f32)
-    even, odd = split_pairs(right)
-    target = tau * pack_pair(even, odd, True) + pulled
+    right_copy.wait()
+    target = tau * (own_right[...] + got_right[...]) + pulled
 
     def load_columns(block):
         first = block // 2
@@ -589,11 +586,12 @@
             pltpu.VMEM((rows, LANES), bf16),
             pltpu.VMEM((rows, LANES), jnp.int32),
             pltpu.VMEM((2, padded, LANES), bf16),
-            pltpu.VMEM((2, padded, LANES), bf16),
+            pltpu.VMEM((padded, LANES), bf16),
             pltpu.VMEM((rows // 2, LANES), bf16),
             pltpu.VMEM((rows // 2, LANES), bf16),
-            pltpu.VMEM((rows // 2, LANES), bf16),
-            pltpu.VMEM((rows // 2, LANES), bf16),
+            pltpu.VMEM((32, LANES), f32),
+            pltpu.VMEM((32, LANES), f32),
+            pltpu.VMEM((32, LANES), f32),
             pltpu.VMEM((LANES, slot_lanes), f32),
             pltpu.VMEM((half_slots + DAY_ROWS, LANES), bf16),
             pltpu.VMEM((half_slots + DAY_ROWS, LANES), bf16),

time: 24.5 us -> 23.1 us (0.943)
  Pallas kernels: 23.8 us -> 22.4 us
    pallas_call x1, Pallas kernels: 23.8 us -> 22.4 us  [paired_shards(): pl.pallas_call(functools.partial(sweep_kernel, tau, days), out_shape=pltp...]
where the time goes in v1:
time: 23.1 us; the launch traced here: 23 us
  Pallas kernels  22.4 us (97%)
  local copies, waits for them, and re-layouts  0.62 us (3%)
    pallas_call x1, Pallas kernels, paired_shards(): pl.pallas_call(functools.partial(sweep_kernel, tau, days), out_shape=pltp...  22.4 us
    unnamed x1, local copies, waits for them, and re-layouts  0.62 us

profile of v1, /device:TPU:0, one launch (start us, length us, event | category | flops | bytes accessed | tf_op | source)
XLA Modules:
  0.0 23.0 jit_solution(4276614476669344498)
XLA Ops:
  0.0 22.4 %sweep_sensors.1 = f32[64,128]{1,0:T(8,128)S(1)} custom-call(bf16[1440,128]{1,0:T(8,128)(2,1)} %y_hbm.1, s32[1440,128]{1,0:T(8,128)} %observed_hbm.1, bf16[5,64]{1,0:T(8,128)(2,1)} %day_hbm.1, bf16[64,144]{1,0:T(8,128)(2,1)} %bitcast.2, bf16[64,128]{1,0:T(8,128)(2,1)} %factor_hbm.1, f32[1,64]{1,0:T(1,128)} %bitcast.3, s32[6,128]{1,0:T(8,128)} %neighbour_hbm.1, ...), custom_call_target="tpu_custom_call" | custom-call | tf_op jit(solution)/shard_map/sweep_sensors/pallas_call | solution.py:573
  22.4 0.6 %copy.11 = f32[64,128]{1,0:T(8,128)} copy(f32[64,128]{1,0:T(8,128)S(1)} %sweep_sensors.1) | data formatting | bytes 65536

commit v2 on v1

--- a/solution.py
+++ b/solution.py
@@ -308,7 +308,6 @@
     features,
     wide_features,
     half_features,
-    outer,
     gram,
     prior_ref,
     noise_own,
@@ -444,14 +443,14 @@
     def gram_block(part, block):
         first = block // 2
         count = COUNTS[block]
-        slab = outer.at[block % 2]
+        tiles = []
         for c in range(8):
             row = wide_features[part, pl.ds(8 * block + c, 1), :]
             row = jnp.broadcast_to(row, (16, padded)).astype(bf16)
             for q in range(first, 4):
-                at = 16 * (c * count + q - first)
-                slab[pl.ds(at, 16), :] = half_features[part, pl.ds(16 * q, 16), :] * row
-        sums = jnp.dot(slab[pl.ds(0, 128 * count), :], mask_ref[part], preferred_element_type=f32)
+                tiles.append(half_features[part, pl.ds(16 * q, 16), :] * row)
+        rows_of_block = jnp.concatenate(tiles, axis=0)
+        sums = jnp.dot(rows_of_block, mask_ref[part], preferred_element_type=f32)
         even, odd = split_pairs(sums)
         return pack_pair(even, odd, True)
 
@@ -599,7 +598,6 @@
             pltpu.VMEM((padded, LANES), f32),
             pltpu.VMEM((2, RANK, padded), f32),
             pltpu.VMEM((2, RANK, padded), bf16),
-            pltpu.VMEM((2, 512, padded), bf16),
             pltpu.VMEM((PACKED_ROWS, LANES), f32),
             pltpu.VMEM((RANK, LANES), f32),
             pltpu.VMEM((RANK, LANES), f32),

time: 23.1 us -> 23.1 us (level)
  no operation moved by 1% of the time
where the time goes in v2:
time: 23.1 us; the launch traced here: 23 us
  Pallas kernels  22.4 us (97%)
  local copies, waits for them, and re-layouts  0.62 us (3%)
    pallas_call x1, Pallas kernels, paired_shards(): pl.pallas_call(functools.partial(sweep_kernel, tau, days), out_shape=pltp...  22.4 us
    unnamed x1, local copies, waits for them, and re-layouts  0.62 us

profile of v2, /device:TPU:0, one launch (start us, length us, event | category | flops | bytes accessed | tf_op | source)
XLA Modules:
  0.0 23.0 jit_solution(3667009797776196944)
XLA Ops:
  0.0 22.4 %sweep_sensors.1 = f32[64,128]{1,0:T(8,128)S(1)} custom-call(bf16[1440,128]{1,0:T(8,128)(2,1)} %y_hbm.1, s32[1440,128]{1,0:T(8,128)} %observed_hbm.1, bf16[5,64]{1,0:T(8,128)(2,1)} %day_hbm.1, bf16[64,144]{1,0:T(8,128)(2,1)} %bitcast.2, bf16[64,128]{1,0:T(8,128)(2,1)} %factor_hbm.1, f32[1,64]{1,0:T(1,128)} %bitcast.3, s32[6,128]{1,0:T(8,128)} %neighbour_hbm.1, ...), custom_call_target="tpu_custom_call" | custom-call | tf_op jit(solution)/shard_map/sweep_sensors/pallas_call | solution.py:572
  22.4 0.6 %copy.11 = f32[64,128]{1,0:T(8,128)} copy(f32[64,128]{1,0:T(8,128)S(1)} %sweep_sensors.1) | data formatting | bytes 65536
